TPU v7x, 32 devices: a whole 2x2x4 slice. The times are simulated.
32 devices in a mesh: tile: 16 (over z, y, x), mode: 2 (over core).
Axes of the slice: x: 2, y: 2, z: 4, core: 2. Of those that a mesh axis runs over, the one named last changes fastest.
Arguments:
- object_field: float32 [2, 4096, 512], P(None, 'tile'), may hold values from -4.2 to 4.2
- probe: float32 [2, 2, 256, 256], P('mode'), may hold values from -2.1 to 2.1
- positions: int32 [2, 32, 2], P(None, 'tile'), may hold values from 0 to 3840, as said below
- measured: float32 [2, 32, 256, 256], P(None, 'tile'), may hold values from 0.1 to 30
Outputs:
- refined_object: float32 [2, 4096, 512], P(None, 'tile')
- refined_probe: float32 [2, 2, 256, 256], P('mode')
Inputs may be any that keep to these rules, and one draw needn't show every extreme that they name: positions[b, j] = (row, column). Position j belongs to tile t = j // 2; its row lies from t * 256 - 256 / 2 to t * 256 - 256 / 2 + 256, both ends reached in some tile, and every pattern lies inside the object of 4096 x 512.
All inputs are finite; a program needn't handle non-finite values.
Results may differ from a plain program's by a relative error of at most 0.0001.
Values sent between devices are 32-bit elements; how exact they have to be, the bound alone decides.
No kernel may reach another device: no remote copies, remote signals or barrier semaphores. Data moves between devices by JAX's collectives and lax.ppermute only.
A program may use at most 64 MiB of HBM per device.

v0:
```python
import functools
import math

import jax
import jax.numpy as jnp
import numpy as np
from jax import lax
from jax.experimental import pallas as pl
from jax.experimental.pallas import tpu as pltpu
from jax.sharding import PartitionSpec as P

F32 = jnp.float32
BF16 = jnp.bfloat16
VMEM_BYTES = 40 * 1024 * 1024


def padded(block, sides, width):
    for axis, dim in sides:
        count = lax.axis_size(axis)
        forward = [(i, i + 1) for i in range(count - 1)]
        backward = [(target, source) for source, target in forward]
        low = lax.ppermute(
            lax.slice_in_dim(block, block.shape[dim] - width, None, axis=dim), axis, forward
        )
        high = lax.ppermute(lax.slice_in_dim(block, 0, width, axis=dim), axis, backward)
        block = jnp.concatenate([low, block, high], axis=dim)
    return block


def tables(length):
    index_values = jnp.arange(length, dtype=jnp.int32)
    product = index_values[:, None] * index_values[None, :] % length
    angles = product.astype(jnp.float32) * (2.0 * math.pi / length)
    scaling = 1.0 / math.sqrt(length)
    return (jnp.cos(angles) * scaling, jnp.sin(angles) * scaling)


def apply_left(matrix, target):
    return jnp.einsum("ab,pbc->pac", matrix, target, precision=lax.Precision.HIGHEST)


def apply_right(target, matrix):
    return jnp.einsum("pab,bc->pac", target, matrix, precision=lax.Precision.HIGHEST)


def transform(real_part, imag_part, cosine, sine_table, direction):
    left_real = apply_left(cosine, real_part) + direction * apply_left(sine_table, imag_part)
    left_imag = apply_left(cosine, imag_part) - direction * apply_left(sine_table, real_part)
    out_real = apply_right(left_real, cosine) + direction * apply_right(left_imag, sine_table)
    out_imag = apply_right(left_imag, cosine) - direction * apply_right(left_real, sine_table)
    return (out_real, out_imag)


def place_add(target, placed, row_start, col_start):
    zero_index = jnp.int32(0)
    current = lax.dynamic_slice(target, (zero_index, row_start, col_start), placed.shape)
    return lax.dynamic_update_slice(target, current + placed, (zero_index, row_start, col_start))


def shards_by_mode(object_field, probe, positions, measured):
    strip_rows = object_field.shape[1]
    object_width = object_field.shape[2]
    pattern = probe.shape[2]
    half_pattern = pattern // 2
    count = positions.shape[1]
    cosine, sine_table = tables(pattern)
    tile_index = lax.axis_index("tile")
    offset = tile_index * strip_rows - half_pattern
    for minibatch in range(measured.shape[0]):
        extended = padded(object_field, (("tile", 1),), half_pattern)
        row_offsets = positions[minibatch, :, 0] - offset
        column_offsets = positions[minibatch, :, 1]

        def cut_one(row_start, col_start):
            return lax.dynamic_slice(
                extended, (jnp.int32(0), row_start, col_start), (2, pattern, pattern)
            )

        patches = jax.vmap(cut_one)(row_offsets, column_offsets)
        obj_real = patches[:, 0]
        obj_imag = patches[:, 1]
        probe_real = probe[0, 0]
        probe_imag = probe[0, 1]
        exit_real = probe_real * obj_real - probe_imag * obj_imag
        exit_imag = probe_real * obj_imag + probe_imag * obj_real
        far_real, far_imag = transform(exit_real, exit_imag, cosine, sine_table, 1.0)
        observed = measured[minibatch]
        intensity = lax.psum(far_real * far_real + far_imag * far_imag, "mode")
        modulus = jnp.sqrt((observed + 1.0) / (intensity + 1.0)) - 1.0
        chi_real, chi_imag = transform(
            modulus * far_real, modulus * far_imag, cosine, sine_table, -1.0
        )
        grad_real = probe_real * chi_real + probe_imag * chi_imag
        grad_imag = probe_real * chi_imag - probe_imag * chi_real
        probe_power = probe_real * probe_real + probe_imag * probe_imag
        step_real = jnp.sum(obj_real * chi_real + obj_imag * chi_imag, axis=0)
        step_imag = jnp.sum(obj_real * chi_imag - obj_imag * chi_real, axis=0)
        coverage = jnp.sum(obj_real * obj_real + obj_imag * obj_imag, axis=0)
        accumulated = jnp.zeros((3, strip_rows + pattern, object_width), jnp.float32)
        for position in range(count):
            placed = jnp.stack([grad_real[position], grad_imag[position], probe_power])
            accumulated = place_add(
                accumulated, placed, row_offsets[position], column_offsets[position]
            )
        rim_rows = jnp.concatenate(
            [accumulated[:, :half_pattern], accumulated[:, strip_rows + half_pattern :]], axis=1
        )
        received = padded(rim_rows, (("tile", 1),), half_pattern)
        own_strip = accumulated[:, half_pattern : half_pattern + strip_rows]
        own_strip = own_strip.at[:, :half_pattern].add(received[:, :half_pattern])
        own_strip = own_strip.at[:, strip_rows - half_pattern :].add(
            received[:, pattern + half_pattern :]
        )
        summed = lax.psum(own_strip, "mode")
        divisor = summed[2] + 1.0
        object_field = jnp.stack(
            [object_field[0] + summed[0] / divisor, object_field[1] + summed[1] / divisor]
        )
        step_stack = jnp.stack([jnp.stack([step_real, step_imag])])
        step_total, coverage_total = lax.psum((step_stack, coverage), "tile")
        probe = probe + step_total / (coverage_total + 1.0)
    return (object_field, probe)


def table_of(length):
    index_values = np.arange(length)
    angles = (index_values[:, None] * index_values[None, :] % length) * (2.0 * np.pi / length)
    scaling = 1.0 / np.sqrt(length)
    return np.stack([np.cos(angles) * scaling, np.sin(angles) * scaling]).astype(np.float32)


def spot(info, size, minibatch, side, slot):
    tiles, strip, pattern = size
    place = (((side + 1) * 2 + minibatch) * 2 + slot) * 2
    tile = info[24]
    row = info[place] - tile * strip + pattern // 2
    if side < 0:
        row = jnp.where(tile == 0, -pattern, row)
    if side > 0:
        row = jnp.where(tile == tiles - 1, strip + pattern, row)
    return row, info[place + 1]


def part_of(ref, part):
    if len(ref.shape) == 3:
        return ref[part]
    return ref[:, part].reshape(ref.shape[0] * ref.shape[2], ref.shape[3])


def take_columns(block, column, width):
    total = block.shape[-1]
    return pltpu.roll(block, lax.rem(total - column, total), 1)[:, :width]


def add_at(tall, block, row, column):
    rows, width = block.shape
    total = tall.shape[1]
    shift = lax.rem(row, 8)
    start = pl.multiple_of(row - shift, 8)
    turned = pltpu.roll(block.reshape(rows // 8, 8, width), shift, 1)
    empty = jnp.zeros((1, 8, width), block.dtype)
    inside = lax.broadcasted_iota(jnp.int32, (rows // 8 + 1, 8, width), 1) >= shift
    moved = jnp.where(
        inside,
        jnp.concatenate([turned, empty], axis=0),
        jnp.concatenate([empty, turned], axis=0),
    ).reshape(rows + 8, width)
    wide = jnp.concatenate([moved, jnp.zeros((rows + 8, total - width), block.dtype)], axis=1)
    tall[pl.ds(start, rows + 8), :] += pltpu.roll(wide, column, 1)


def rows_at(ref, row, rows):
    width = ref.shape[1]
    shift = lax.rem(row, 8)
    start = pl.multiple_of(row - shift, 8)
    block = ref[pl.ds(start, rows + 8), :].reshape(rows // 8 + 1, 8, width)
    turned = pltpu.roll(block, lax.rem(8 - shift, 8), 1)
    inside = lax.broadcasted_iota(jnp.int32, (rows // 8, 8, width), 1) < 8 - shift
    return jnp.where(inside, turned[:-1], turned[1:]).reshape(rows, width)


def halves(value):
    high = value.astype(BF16)
    return high, (value - high.astype(F32)).astype(BF16)


def product(left, right):
    dot = functools.partial(jnp.dot, preferred_element_type=F32)
    return dot(left[0], right[0]) + (dot(left[0], right[1]) + dot(left[1], right[0]))


def cut_patch(size, info, minibatch, strip_ref, below, above, window, part):
    tiles, rows, width = size
    half = width // 2
    row, column = spot(info, size, minibatch, 0, info[25])

    def columns(block):
        return block if block.shape[1] == width else take_columns(block, column, width)

    window[:half] = columns(below)
    window[half : half + rows] = columns(strip_ref[part])
    window[half + rows : rows + width] = columns(above)
    return rows_at(window, row, width)


def illumination_kernel(size, minibatch, info, own, other, out, tall):
    tiles, strip, pattern = size
    half = pattern // 2
    kept = slice(pattern + half, pattern + half + strip)
    tall[kept] = jnp.zeros((strip, tall.shape[1]), F32)
    (pr0, pi0), (pr1, pi1) = ((part_of(ref, 0), part_of(ref, 1)) for ref in (own, other))
    power = pr0 * pr0 + pi0 * pi0 + (pr1 * pr1 + pi1 * pi1)
    for side in (-1, 0, 1):
        for slot in range(2):
            row, column = spot(info, size, minibatch, side, slot)
            add_at(tall, power, row + pattern, column)
    out[...] = tall[kept]


def field_kernel(size, minibatch, info, strip_ref, *refs):
    edges, (own, other, measured, table) = refs[:-10], refs[-10:-6]
    gradient, step_own, step_other, window, observed, arrived = refs[-6:]
    tiles, strip, pattern = size
    slot = info[25]
    fetch = pltpu.make_async_copy(measured.at[minibatch, slot], observed, arrived)
    fetch.start()
    (cos_high, cos_low), (sin_high, sin_low) = halves(table[0]), halves(table[1])

    def block(top_left, top_right, low_left, low_right):
        return jnp.concatenate(
            [
                jnp.concatenate([top_left, top_right], axis=1),
                jnp.concatenate([low_left, low_right], axis=1),
            ],
            axis=0,
        )

    first = (
        block(cos_high, sin_high, -sin_high, cos_high),
        block(cos_low, sin_low, -sin_low, cos_low),
    )
    second = (
        block(cos_high, -sin_high, sin_high, cos_high),
        block(cos_low, -sin_low, sin_low, cos_low),
    )
    def edge(side, part):
        if len(edges) == 2:
            return edges[side][part]
        return jnp.where(slot == part, edges[2 * side][...], edges[2 * side + 1][...])

    obj_real, obj_imag = (
        cut_patch(size, info, minibatch, strip_ref, edge(0, part), edge(1, part), window, part)
        for part in range(2)
    )
    probes = [(part_of(ref, 0), part_of(ref, 1)) for ref in (own, other)]

    def both(fields, left, right):
        (r0, i0), (r1, i1) = fields
        y = product(left, halves(block(r0, r1, i0, i1)))
        y = block(
            y[:pattern, :pattern], y[pattern:, :pattern], y[:pattern, pattern:], y[pattern:, pattern:]
        )
        y = product(halves(y), right)
        return (
            (y[:pattern, :pattern], y[:pattern, pattern:]),
            (y[pattern:, :pattern], y[pattern:, pattern:]),
        )

    exits = [(pr * obj_real - pi * obj_imag, pr * obj_imag + pi * obj_real) for pr, pi in probes]
    far = both(exits, first, second)
    intensity = (far[0][0] * far[0][0] + far[0][1] * far[0][1]) + (
        far[1][0] * far[1][0] + far[1][1] * far[1][1]
    )
    fetch.wait()
    factor = jnp.sqrt((observed[...] + 1.0) / (intensity + 1.0)) - 1.0
    chi = both([(factor * fr, factor * fi) for fr, fi in far], second, first)
    (pr0, pi0), (pr1, pi1) = probes
    (cr0, ci0), (cr1, ci1) = chi
    gradient[0] = (pr0 * cr0 + pi0 * ci0) + (pr1 * cr1 + pi1 * ci1)
    gradient[1] = (pr0 * ci0 - pi0 * cr0) + (pr1 * ci1 - pi1 * cr1)
    coverage = obj_real * obj_real + obj_imag * obj_imag
    rows = pattern // tiles
    for step, (cr, ci) in ((step_own, chi[0]), (step_other, chi[1])):
        for part, value in (
            (0, obj_real * cr + obj_imag * ci),
            (1, obj_real * ci - obj_imag * cr),
            (2, coverage),
        ):
            step[:, part] = value.reshape(tiles, rows, pattern)


def update_kernel(size, minibatch, info, strip_ref, illum, own, other, b0, a0, b1, a1, *outs):
    strip_out, *edges, tall = outs
    tiles, strip, pattern = size
    half = pattern // 2
    slot = info[25]
    kept = slice(pattern + half, pattern + half + strip)
    grads = (
        (0, slot, own, 0),
        (0, 1 - slot, other, 0),
        (-1, slot, b0, half),
        (1, slot, a0, 0),
        (-1, 1 - slot, b1, half),
        (1, 1 - slot, a1, 0),
    )
    for part in range(2):
        tall[kept] = jnp.zeros((strip, tall.shape[1]), F32)
        for side, place, ref, start in grads:
            row, column = spot(info, size, minibatch, side, place)
            add_at(tall, ref[part], row + pattern + start, column)
        fresh = strip_ref[part] + tall[kept] / (illum[...] + 1.0)
        strip_out[part] = fresh
        if edges:
            column_below = spot(info, size, minibatch + 1, -1, slot)[1]
            column_above = spot(info, size, minibatch + 1, 1, slot)[1]
            edges[0][part] = take_columns(fresh[:half], column_below, pattern)
            edges[1][part] = take_columns(fresh[strip - half :], column_above, pattern)


def piece_kernel(info, sums, probe, out):
    tiles, parts, rows, width = sums.shape
    tile = info[24]
    total = sums[0]
    for k in range(1, tiles):
        total += sums[k]
    divisor = total[2] + 1.0
    for part in range(2):
        if len(probe.shape) == 3:
            held = probe[part, pl.ds(pl.multiple_of(tile * rows, rows), rows), :]
        else:
            held = probe[tile, part]
        fresh = held + total[part] / divisor
        for k in range(tiles):
            out[k, part] = fresh


def gather_kernel(info, blocks, out):
    for part in range(2):
        out[part] = part_of(blocks, part)


def call(kernel, name, outs, inputs, scratch=(), flops=0, far=None):
    shapes = [jax.ShapeDtypeStruct(shape, F32) for shape in outs]
    size = 4 * sum(math.prod(shape) for shape in outs) + sum(
        value.size * value.dtype.itemsize for value in inputs
    )
    smem = pl.BlockSpec(memory_space=pltpu.SMEM)
    vmem = pl.BlockSpec(memory_space=pltpu.VMEM)
    return pl.pallas_call(
        kernel,
        out_shape=shapes,
        in_specs=[smem]
        + [pl.BlockSpec(memory_space=pl.ANY) if value is far else vmem for value in inputs[1:]],
        out_specs=[vmem] * len(shapes),
        scratch_shapes=[pltpu.VMEM(shape, F32) for shape in scratch]
        + ([] if far is None else [pltpu.SemaphoreType.DMA]),
        compiler_params=pltpu.CompilerParams(vmem_limit_bytes=VMEM_BYTES),
        cost_estimate=pl.CostEstimate(flops=flops, bytes_accessed=size, transcendentals=0),
        name=name,
    )(*inputs)


def shards_by_position(object_field, probe, positions, measured):
    strip = object_field.shape[1]
    width = object_field.shape[2]
    pattern = probe.shape[2]
    half = pattern // 2
    tiles = lax.axis_size("tile")
    size = (tiles, strip, pattern)
    field = (2, pattern, pattern)
    tall = (3 * pattern + strip + 8, width)
    window = (pattern + strip + 8, pattern)
    up = [(i, i + 1) for i in range(tiles - 1)]
    down = [(i + 1, i) for i in range(tiles - 1)]

    def swap(value):
        return lax.ppermute(value, "mode", [(0, 1), (1, 0)])

    def to_all(blocks):
        return lax.all_to_all(blocks, "tile", 0, 0, tiled=True)

    def from_below(value):
        return lax.ppermute(value, "tile", up)

    def from_above(value):
        return lax.ppermute(value, "tile", down)

    def bind(kernel, *args):
        return functools.partial(kernel, *args)

    table = jnp.asarray(table_of(pattern))
    tile, slot = lax.axis_index("tile"), lax.axis_index("mode")
    one_part = lax.dynamic_index_in_dim(object_field, slot, 0, keepdims=False)
    edges = [from_below(one_part[strip - half :]), from_above(one_part[:half])]
    edges = [edges[0], swap(edges[0]), edges[1], swap(edges[1])]
    index = jnp.stack([tile, slot]).astype(jnp.int32)
    below, above = from_below(positions), from_above(positions)
    here = jnp.concatenate([positions.ravel()] * 3 + [index])
    info = jnp.concatenate([below.ravel(), positions.ravel(), above.ravel(), index])
    own = probe[0]
    other = swap(own)

    for minibatch in range(2):
        blocks = (tiles, 3, pattern // tiles, pattern)
        gradient, step_own, step_other = call(
            bind(field_kernel, size, minibatch),
            "field",
            [field, blocks, blocks],
            (here, object_field, *edges, own, other, measured, table),
            [window, (pattern, pattern)],
            flops=2 * 12 * 512**3,
            far=measured,
        )
        (illum,) = call(
            bind(illumination_kernel, size, minibatch),
            "illumination",
            [(strip, width)],
            (info, own, other),
            [tall],
        )
        rim_below, rim_above = from_below(gradient[:, half:]), from_above(gradient[:, :half])
        rims = (gradient, swap(gradient), rim_below, rim_above, swap(rim_below), swap(rim_above))
        last = minibatch == 1
        object_field, *edges = call(
            bind(update_kernel, size, minibatch),
            "update",
            [object_field.shape] + ([] if last else [(2, half, pattern)] * 2),
            (info, object_field, illum, *rims),
            [tall],
        )
        if not last:
            edges = [from_below(edges[1]), from_above(edges[0])]

        sums = to_all(step_own + swap(step_other))
        (fresh,) = call(
            piece_kernel, "piece", [(tiles, 2, pattern // tiles, pattern)], (here, sums, own)
        )
        own = to_all(fresh)
        if not last:
            other = swap(own)
    (own,) = call(gather_kernel, "gather", [field], (here, own))
    return (object_field, own[None])


def solution(mesh):
    in_specs = (
        P(None, "tile", None),
        P("mode", None, None, None),
        P(None, "tile", None),
        P(None, "tile", None, None),
    )
    out_specs = (P(None, "tile", None), P("mode", None, None, None))

    def whole(object_field, probe, positions, measured):
        tiles, pair = mesh.shape["tile"], mesh.shape["mode"]
        by_position = (
            pair == 2
            and probe.shape[0] == 2
            and positions.shape[:2] == (2, 2 * tiles)
            and probe.shape[2] % (8 * tiles) == 0
            and object_field.shape[1] == tiles * probe.shape[2]
        )
        shards = shards_by_position if by_position else shards_by_mode
        return jax.shard_map(
            shards, mesh=mesh, in_specs=in_specs, out_specs=out_specs, check_vma=False
        )(object_field, probe, positions, measured)

    return whole
```

profile of v0, /device:TPU:0, one launch (start us, length us, event | category | flops | bytes accessed | tf_op | source)
XLA Modules:
  0.0 184.9 jit_solution(18410107580920813187)
XLA Ops:
  0.6 1.2 dynamic-slice_bitcast_fusion
  1.8 4.9 %collective-permute-start.3 = (f32[128,512]{1,0:T(8,128)S(1)}, f32[128,512]{1,0:T(8,128)S(1)}, u32[]{:S(2)}, u32[]{:S(2)}) collective-permute-start(f32[128,512]{1,0:T(8,128)S(1)} %get-tuple-element.21), channel_id=1, source_target_pairs={{0,2},{2,4},{4,6},{6,8},{8,10},{10,12},{12,14},{14,16},{16,18},{18... | collective-permute-start | bytes 786440 | tf_op jit(solution)/shard_map/ppermute | solution.py:383
  6.7 1.3 collective-permute-start.5
  8.0 9.8 %collective-permute-done.3.refs_0_ = f32[128,512]{1,0:T(8,128)S(1)} collective-permute-done((f32[128,512]{1,0:T(8,128)S(1)}, f32[128,512]{1,0:T(8,128)S(1)}, u32[]{:S(2)}, u32[]{:S(2)}) %collective-permute-start.3) | collective-permute-done | bytes 262176 | tf_op jit(solution)/shard_map/ppermute | solution.py:383
  17.9 1.9 %collective-permute-done.5.refs_2_ = f32[128,512]{1,0:T(8,128)S(1)} collective-permute-done((f32[128,512]{1,0:T(8,128)S(1)}, f32[128,512]{1,0:T(8,128)S(1)}, u32[]{:S(2)}, u32[]{:S(2)}) %collective-permute-start.5) | collective-permute-done | bytes 262176 | tf_op jit(solution)/shard_map/ppermute | solution.py:386
  19.8 0.7 copy-done.9
  20.4 0.1 reshape.17
  20.5 0.1 concatenate.9.info
  20.6 0.7 collective-permute-done.6.refs_3_
  21.3 1.0 copy-done.1
  22.4 1.2 copy-done.5
  23.6 1.0 copy-done.7
  24.6 5.4 %field.2 = (f32[2,256,256]{2,1,0:T(8,128)S(1)}, f32[16,3,16,256]{3,2,1,0:T(8,128)S(1)}, f32[16,3,16,256]{3,2,1,0:T(8,128)S(1)}) custom-call(s32[26]{0:T(128)S(1)} %concatenate.9.info, f32[2,256,512]{2,1,0:T(8,128)S(1)} %copy-done, f32[128,512]{1,0:T(8,128)S(1)} %collective-permute-done.3.refs_0_, f32[128,512]{1,0:T(8,128)S(1)} %collective-permute-done.4.refs_1_, ...), custom_call_target="tpu_custom_call" | custom-call | flops 3221225472 | bytes 6815848 | tf_op jit(solution)/shard_map/field/pallas_call | solution.py:349
  30.0 0.2 collective-permute-start.12
  30.2 2.1 %collective-permute-done.12 = f32[16,3,16,256]{3,2,1,0:T(8,128)S(1)} collective-permute-done((f32[16,3,16,256]{3,2,1,0:T(8,128)S(1)}, f32[16,3,16,256]{3,2,1,0:T(8,128)S(1)}, u32[]{:S(2)}, u32[]{:S(2)}) %collective-permute-start.12) | collective-permute-done | bytes 786464 | tf_op jit(solution)/shard_map/ppermute | solution.py:377
  32.3 0.1 add.11
  32.5 27.3 %all_to_all.20.sums = f32[16,3,16,256]{3,2,1,0:T(8,128)S(1)} all-to-all(f32[16,3,16,256]{3,2,1,0:T(8,128)S(1)} %add.11), channel_id=1, replica_groups=mesh['tile'=16,'mode'=2] {'tile'}, dimensions={0} | all-to-all | bytes 1572864 | tf_op jit(solution)/shard_map/all_to_all | solution.py:380
  59.8 1.4 piece.2
  61.2 3.6 %all-to-all-start.1 = ((f32[16,2,16,256]{3,2,1,0:T(8,128)}), f32[16,2,16,256]{3,2,1,0:T(8,128)S(1)}, u32[]{:S(2)}, u32[]{:S(2)}) async-start(f32[16,2,16,256]{3,2,1,0:T(8,128)} %piece.2), calls=%async_computation.1 | async-start | bytes 1048576 | tf_op jit(solution)/shard_map/all_to_all | solution.py:380
  64.8 3.9 %collective-permute-start.8 = (f32[2,128,256]{2,1,0:T(8,128)S(1)}, f32[2,128,256]{2,1,0:T(8,128)S(1)}, u32[]{:S(2)}, u32[]{:S(2)}) collective-permute-start(f32[2,128,256]{2,1,0:T(8,128)S(1)} %get-tuple-element.25), channel_id=1, source_target_pairs={{0,2},{2,4},{4,6},{6,8},{8,10},{10,12},{12,14},{14,16},{16,18},{18... | collective-permute-start | bytes 786440 | tf_op jit(solution)/shard_map/ppermute | solution.py:383
  68.7 1.3 collective-permute-start.9
  70.1 12.3 %collective-permute-done.8.b0 = f32[2,128,256]{2,1,0:T(8,128)S(1)} collective-permute-done((f32[2,128,256]{2,1,0:T(8,128)S(1)}, f32[2,128,256]{2,1,0:T(8,128)S(1)}, u32[]{:S(2)}, u32[]{:S(2)}) %collective-permute-start.8) | collective-permute-done | bytes 262176 | tf_op jit(solution)/shard_map/ppermute | solution.py:383
  82.4 2.2 %collective-permute-done.9.a0 = f32[2,128,256]{2,1,0:T(8,128)} collective-permute-done((f32[2,128,256]{2,1,0:T(8,128)S(1)}, f32[2,128,256]{2,1,0:T(8,128)}, u32[]{:S(2)}, u32[]{:S(2)}) %collective-permute-start.9) | collective-permute-done | bytes 262176 | tf_op jit(solution)/shard_map/ppermute | solution.py:386
  84.6 0.5 collective-permute-start.13
  85.1 3.2 %collective-permute-start = (s32[2,2,2]{2,1,0:T(2,128)S(1)}, s32[2,2,2]{2,1,0:T(2,128)S(1)}, u32[]{:S(2)}, u32[]{:S(2)}) collective-permute-start(s32[2,2,2]{2,1,0:T(2,128)S(1)} %copy-done.9), channel_id=1, source_target_pairs={{0,2},{2,4},{4,6},{6,8},{8,10},{10,12},{12,14},{14,16},{16,18},{18... | collective-permute-start | bytes 104 | tf_op jit(solution)/shard_map/ppermute | solution.py:383
  88.3 1.3 collective-permute-done
  89.6 1.3 collective-permute-start.1
  90.9 0.1 reshape.16
  90.9 4.4 %collective-permute-done.1 = s32[2,2,2]{2,1,0:T(2,128)S(1)} collective-permute-done((s32[2,2,2]{2,1,0:T(2,128)S(1)}, s32[2,2,2]{2,1,0:T(2,128)S(1)}, u32[]{:S(2)}, u32[]{:S(2)}) %collective-permute-start.1) | collective-permute-done | bytes 64 | tf_op jit(solution)/shard_map/ppermute | solution.py:386
  95.5 1.7 illumination.2.illum
  97.2 3.2 %update.2 = (f32[2,256,512]{2,1,0:T(8,128)S(1)}, f32[2,128,256]{2,1,0:T(8,128)S(1)}, f32[2,128,256]{2,1,0:T(8,128)S(1)}) custom-call(s32[26]{0:T(128)S(1)} %concatenate.8.info, f32[2,256,512]{2,1,0:T(8,128)S(1)} %copy-done, f32[256,512]{1,0:T(8,128)S(1)} %illumination.2.illum, f32[2,256,256]{2,1,0:T(8,128)S(1)} %get-tuple-element.11.own, ...), custom_call_target="tpu_custom_call" | custom-call | bytes 5242984 | tf_op jit(solution)/shard_map/update/pallas_call | solution.py:349
  100.4 4.8 %collective-permute-start.14 = (f32[2,128,256]{2,1,0:T(8,128)S(1)}, f32[2,128,256]{2,1,0:T(8,128)S(1)}, u32[]{:S(2)}, u32[]{:S(2)}) collective-permute-start(f32[2,128,256]{2,1,0:T(8,128)S(1)} %get-tuple-element.15), channel_id=1, source_target_pairs={{0,2},{2,4},{4,6},{6,8},{8,10},{10,12},{12,14},{14,16},{16,18},{18... | collective-permute-start | bytes 786440 | tf_op jit(solution)/shard_map/ppermute | solution.py:383
  105.2 1.3 collective-permute-start.15
  106.5 2.6 %collective-permute-done.14.refs_0_ = f32[2,128,256]{2,1,0:T(8,128)S(1)} collective-permute-done((f32[2,128,256]{2,1,0:T(8,128)S(1)}, f32[2,128,256]{2,1,0:T(8,128)S(1)}, u32[]{:S(2)}, u32[]{:S(2)}) %collective-permute-start.14) | collective-permute-done | bytes 262176 | tf_op jit(solution)/shard_map/ppermute | solution.py:383
  109.1 6.1 %collective-permute-done.15.refs_1_ = f32[2,128,256]{2,1,0:T(8,128)S(1)} collective-permute-done((f32[2,128,256]{2,1,0:T(8,128)S(1)}, f32[2,128,256]{2,1,0:T(8,128)S(1)}, u32[]{:S(2)}, u32[]{:S(2)}) %collective-permute-start.15) | collective-permute-done | bytes 262176 | tf_op jit(solution)/shard_map/ppermute | solution.py:386
  115.2 5.5 %field.3 = (f32[2,256,256]{2,1,0:T(8,128)S(1)}, f32[16,3,16,256]{3,2,1,0:T(8,128)S(1)}, f32[16,3,16,256]{3,2,1,0:T(8,128)S(1)}) custom-call(s32[26]{0:T(128)S(1)} %concatenate.9.info, f32[2,256,512]{2,1,0:T(8,128)S(1)} %get-tuple-element.12.strip_ref, f32[2,128,256]{2,1,0:T(8,128)S(1)} %collective-permute-done.14.refs_0_, ...), custom_call_target="tpu_custom_call" | custom-call | flops 3221225472 | bytes 6291560 | tf_op jit(solution)/shard_map/field/pallas_call | solution.py:349
  120.8 2.3 %collective-permute-done.21 = f32[16,3,16,256]{3,2,1,0:T(8,128)S(1)} collective-permute-done((f32[16,3,16,256]{3,2,1,0:T(8,128)S(1)}, f32[16,3,16,256]{3,2,1,0:T(8,128)S(1)}, u32[]{:S(2)}, u32[]{:S(2)}) %collective-permute-start.21) | collective-permute-done | bytes 786464 | tf_op jit(solution)/shard_map/ppermute | solution.py:377
  123.1 0.1 add.12
  123.2 29.0 %all_to_all.21.sums = f32[16,3,16,256]{3,2,1,0:T(8,128)S(1)} all-to-all(f32[16,3,16,256]{3,2,1,0:T(8,128)S(1)} %add.12), channel_id=1, replica_groups=mesh['tile'=16,'mode'=2] {'tile'}, dimensions={0} | all-to-all | bytes 1572864 | tf_op jit(solution)/shard_map/all_to_all | solution.py:380
  152.3 1.4 piece.3
  153.7 3.6 %all-to-all-start.3 = ((f32[16,2,16,256]{3,2,1,0:T(8,128)}), f32[16,2,16,256]{3,2,1,0:T(8,128)S(1)}, u32[]{:S(2)}, u32[]{:S(2)}) async-start(f32[16,2,16,256]{3,2,1,0:T(8,128)} %piece.3), calls=%async_computation.3 | async-start | bytes 1048576 | tf_op jit(solution)/shard_map/all_to_all | solution.py:380
  157.4 3.8 %collective-permute-start.17 = (f32[2,128,256]{2,1,0:T(8,128)S(1)}, f32[2,128,256]{2,1,0:T(8,128)S(1)}, u32[]{:S(2)}, u32[]{:S(2)}) collective-permute-start(f32[2,128,256]{2,1,0:T(8,128)S(1)} %get-tuple-element.23), channel_id=1, source_target_pairs={{0,2},{2,4},{4,6},{6,8},{8,10},{10,12},{12,14},{14,16},{16,18},{18... | collective-permute-start | bytes 786440 | tf_op jit(solution)/shard_map/ppermute | solution.py:383
  161.2 1.3 collective-permute-start.18
  162.5 13.8 %collective-permute-done.17.b0 = f32[2,128,256]{2,1,0:T(8,128)S(1)} collective-permute-done((f32[2,128,256]{2,1,0:T(8,128)S(1)}, f32[2,128,256]{2,1,0:T(8,128)S(1)}, u32[]{:S(2)}, u32[]{:S(2)}) %collective-permute-start.17) | collective-permute-done | bytes 262176 | tf_op jit(solution)/shard_map/ppermute | solution.py:383
  176.3 1.9 %collective-permute-done.18.a0 = f32[2,128,256]{2,1,0:T(8,128)S(1)} collective-permute-done((f32[2,128,256]{2,1,0:T(8,128)S(1)}, f32[2,128,256]{2,1,0:T(8,128)S(1)}, u32[]{:S(2)}, u32[]{:S(2)}) %collective-permute-start.18) | collective-permute-done | bytes 262176 | tf_op jit(solution)/shard_map/ppermute | solution.py:386
  178.2 2.2 %illumination.3.illum = f32[256,512]{1,0:T(8,128)S(1)} custom-call(s32[26]{0:T(128)S(1)} %concatenate.8.info, f32[16,2,16,256]{3,2,1,0:T(8,128)S(1)} %all-to-all-done.1.own.refs_2_.probe, f32[16,2,16,256]{3,2,1,0:T(8,128)} %collective-permute-done.13.other.refs_3_), custom_call_target="tpu_custom_call" | custom-call | bytes 1572968 | tf_op jit(solution)/shard_map/illumination/pallas_call | solution.py:349
  180.4 3.1 %update.3 = f32[2,256,512]{2,1,0:T(8,128)} custom-call(s32[26]{0:T(128)S(1)} %concatenate.8.info, f32[2,256,512]{2,1,0:T(8,128)S(1)} %copy-done.4, f32[256,512]{1,0:T(8,128)S(1)} %illumination.3.illum, f32[2,256,256]{2,1,0:T(8,128)S(1)} %get-tuple-element.17.own, f32[2,256,256]{2,1,0:T(8,128)S(1)} %collective-permute-done.16.other, ...), custom_call_target="tpu_custom_call" | custom-call | bytes 4718696 | tf_op jit(solution)/shard_map/update/pallas_call | solution.py:349
  183.5 1.4 gather.1
  (41 shorter events, 0.6 us)
Async XLA Ops:
  0.6 20.7 %copy-start = (f32[2,256,512]{2,1,0:T(8,128)S(1)}, f32[2,256,512]{2,1,0:T(8,128)}, u32[]{:S(2)}) copy-start(f32[2,256,512]{2,1,0:T(8,128)} %strip_ref.3) | copy-start | bytes 3145732
  1.8 16.0 %collective-permute-start.3 = (f32[128,512]{1,0:T(8,128)S(1)}, f32[128,512]{1,0:T(8,128)S(1)}, u32[]{:S(2)}, u32[]{:S(2)}) collective-permute-start(f32[128,512]{1,0:T(8,128)S(1)} %get-tuple-element.21), channel_id=1, source_target_pairs={{0,2},{2,4},{4,6},{6,8},{8,10},{10,12},{12,14},{14,16},{16,18},{18... | collective-permute-start | bytes 786440 | tf_op jit(solution)/shard_map/ppermute | solution.py:383
  6.7 13.1 %collective-permute-start.5 = (f32[128,512]{1,0:T(8,128)S(1)}, f32[128,512]{1,0:T(8,128)S(1)}, u32[]{:S(2)}, u32[]{:S(2)}) collective-permute-start(f32[128,512]{1,0:T(8,128)S(1)} %get-tuple-element.20), channel_id=1, source_target_pairs={{2,0},{4,2},{6,4},{8,6},{10,8},{12,10},{14,12},{16,14},{18,16},{20... | collective-permute-start | bytes 786440 | tf_op jit(solution)/shard_map/ppermute | solution.py:386
  8.0 13.3 %collective-permute-start.2 = (f32[2,256,256]{2,1,0:T(8,128)}, f32[2,256,256]{2,1,0:T(8,128)S(1)}, u32[]{:S(2)}, u32[]{:S(2)}) collective-permute-start(f32[2,256,256]{2,1,0:T(8,128)} %bitcast.8), channel_id=1, source_target_pairs={{0,1},{1,0},{2,3},{3,2},{4,5},{5,4},{6,7},{7,6},{8,9},{9,8},{10,11... | collective-permute-start | bytes 1572872 | tf_op jit(solution)/shard_map/ppermute | solution.py:377
  17.8 2.8 %collective-permute-start.4 = (f32[128,512]{1,0:T(8,128)S(1)}, f32[128,512]{1,0:T(8,128)S(1)}, u32[]{:S(2)}, u32[]{:S(2)}) collective-permute-start(f32[128,512]{1,0:T(8,128)S(1)} %collective-permute-done.3.refs_0_), channel_id=1, source_target_pairs={{0,1},{1,0},{2,3},{3,2},{4,5},{5,4},{6,7},{7,6},{8,9},{9,8},{10,11... | collective-permute-start | bytes 786440 | tf_op jit(solution)/shard_map/ppermute | solution.py:377
  19.8 1.5 collective-permute-start.6
  19.8 0.7 copy-start.9
  21.3 1.0 copy-start.1
  22.3 1.2 copy-start.5
  23.6 1.0 copy-start.7
  30.0 2.4 %collective-permute-start.12 = (f32[16,3,16,256]{3,2,1,0:T(8,128)S(1)}, f32[16,3,16,256]{3,2,1,0:T(8,128)S(1)}, u32[]{:S(2)}, u32[]{:S(2)}) collective-permute-start(f32[16,3,16,256]{3,2,1,0:T(8,128)S(1)} %get-tuple-element.14), channel_id=1, source_target_pairs={{0,1},{1,0},{2,3},{3,2},{4,5},{5,4},{6,7},{7,6},{8,9},{9,8},{10,11... | collective-permute-start | bytes 2359304 | tf_op jit(solution)/shard_map/ppermute | solution.py:377
  61.2 23.4 %all-to-all-start.1 = ((f32[16,2,16,256]{3,2,1,0:T(8,128)}), f32[16,2,16,256]{3,2,1,0:T(8,128)S(1)}, u32[]{:S(2)}, u32[]{:S(2)}) async-start(f32[16,2,16,256]{3,2,1,0:T(8,128)} %piece.2), calls=%async_computation.1 | async-start | bytes 1048576 | tf_op jit(solution)/shard_map/all_to_all | solution.py:380
  64.8 30.7 %copy-start.2 = (f32[1,2,256,256]{3,2,1,0:T(8,128)S(1)}, f32[1,2,256,256]{3,2,1,0:T(8,128)}, u32[]{:S(2)}) copy-start(f32[1,2,256,256]{3,2,1,0:T(8,128)} %param.6) | copy-start | bytes 1572868
  64.8 17.5 %collective-permute-start.8 = (f32[2,128,256]{2,1,0:T(8,128)S(1)}, f32[2,128,256]{2,1,0:T(8,128)S(1)}, u32[]{:S(2)}, u32[]{:S(2)}) collective-permute-start(f32[2,128,256]{2,1,0:T(8,128)S(1)} %get-tuple-element.25), channel_id=1, source_target_pairs={{0,2},{2,4},{4,6},{6,8},{8,10},{10,12},{12,14},{14,16},{16,18},{18... | collective-permute-start | bytes 786440 | tf_op jit(solution)/shard_map/ppermute | solution.py:383
  68.7 15.9 %collective-permute-start.9 = (f32[2,128,256]{2,1,0:T(8,128)S(1)}, f32[2,128,256]{2,1,0:T(8,128)}, u32[]{:S(2)}, u32[]{:S(2)}) collective-permute-start(f32[2,128,256]{2,1,0:T(8,128)S(1)} %get-tuple-element.24), channel_id=1, source_target_pairs={{2,0},{4,2},{6,4},{8,6},{10,8},{12,10},{14,12},{16,14},{18,16},{20... | collective-permute-start | bytes 786440 | tf_op jit(solution)/shard_map/ppermute | solution.py:386
  70.0 27.2 %collective-permute-start.7 = (f32[2,256,256]{2,1,0:T(8,128)S(1)}, f32[2,256,256]{2,1,0:T(8,128)}, u32[]{:S(2)}, u32[]{:S(2)}) collective-permute-start(f32[2,256,256]{2,1,0:T(8,128)S(1)} %get-tuple-element.11.own), channel_id=1, source_target_pairs={{0,1},{1,0},{2,3},{3,2},{4,5},{5,4},{6,7},{7,6},{8,9},{9,8},{10,11... | collective-permute-start | bytes 1572872 | tf_op jit(solution)/shard_map/ppermute | solution.py:377
  82.4 14.8 %collective-permute-start.10 = (f32[2,128,256]{2,1,0:T(8,128)S(1)}, f32[2,128,256]{2,1,0:T(8,128)}, u32[]{:S(2)}, u32[]{:S(2)}) collective-permute-start(f32[2,128,256]{2,1,0:T(8,128)S(1)} %collective-permute-done.8.b0), channel_id=1, source_target_pairs={{0,1},{1,0},{2,3},{3,2},{4,5},{5,4},{6,7},{7,6},{8,9},{9,8},{10,11... | collective-permute-start | bytes 786440 | tf_op jit(solution)/shard_map/ppermute | solution.py:377
  84.6 12.6 %collective-permute-start.11 = (f32[2,128,256]{2,1,0:T(8,128)}, f32[2,128,256]{2,1,0:T(8,128)}, u32[]{:S(2)}, u32[]{:S(2)}) collective-permute-start(f32[2,128,256]{2,1,0:T(8,128)} %collective-permute-done.9.a0), channel_id=1, source_target_pairs={{0,1},{1,0},{2,3},{3,2},{4,5},{5,4},{6,7},{7,6},{8,9},{9,8},{10,11... | collective-permute-start | bytes 786440 | tf_op jit(solution)/shard_map/ppermute | solution.py:377
  84.6 30.6 %collective-permute-start.13 = (f32[16,2,16,256]{3,2,1,0:T(8,128)S(1)}, f32[16,2,16,256]{3,2,1,0:T(8,128)}, u32[]{:S(2)}, u32[]{:S(2)}) collective-permute-start(f32[16,2,16,256]{3,2,1,0:T(8,128)S(1)} %all-to-all-done.1.own.refs_2_.probe), channel_id=1, source_target_pairs={{0,1},{1,0},{2,3},{3,2},{4,5},{5,4},{6,7},{7,6},{8,9},{9,8},{10,11... | collective-permute-start | bytes 1572872 | tf_op jit(solution)/shard_map/ppermute | solution.py:377
  85.1 4.5 %collective-permute-start = (s32[2,2,2]{2,1,0:T(2,128)S(1)}, s32[2,2,2]{2,1,0:T(2,128)S(1)}, u32[]{:S(2)}, u32[]{:S(2)}) collective-permute-start(s32[2,2,2]{2,1,0:T(2,128)S(1)} %copy-done.9), channel_id=1, source_target_pairs={{0,2},{2,4},{4,6},{6,8},{8,10},{10,12},{12,14},{14,16},{16,18},{18... | collective-permute-start | bytes 104 | tf_op jit(solution)/shard_map/ppermute | solution.py:383
  89.6 5.7 %collective-permute-start.1 = (s32[2,2,2]{2,1,0:T(2,128)S(1)}, s32[2,2,2]{2,1,0:T(2,128)S(1)}, u32[]{:S(2)}, u32[]{:S(2)}) collective-permute-start(s32[2,2,2]{2,1,0:T(2,128)S(1)} %copy-done.9), channel_id=1, source_target_pairs={{2,0},{4,2},{6,4},{8,6},{10,8},{12,10},{14,12},{16,14},{18,16},{20... | collective-permute-start | bytes 104 | tf_op jit(solution)/shard_map/ppermute | solution.py:386
  97.1 18.0 %copy-start.6 = (f32[2,2,256,256]{3,2,1,0:T(8,128)S(1)}, f32[2,2,256,256]{3,2,1,0:T(8,128)}, u32[]{:S(2)}) copy-start(f32[2,2,256,256]{3,2,1,0:T(8,128)} %refs_4_.1) | copy-start | bytes 3145732
  97.1 18.0 %copy-start.8 = (f32[2,256,256]{2,1,0:T(8,128)S(1)}, f32[2,256,256]{2,1,0:T(8,128)}, u32[]{:S(2)}) copy-start(f32[2,256,256]{2,1,0:T(8,128)} %constant.16.clone.refs_7_.refs_5_) | copy-start | bytes 1572868
  100.4 20.4 %copy-start.3 = (f32[2,256,512]{2,1,0:T(8,128)}, f32[2,256,512]{2,1,0:T(8,128)S(1)}, u32[]{:S(2)}) copy-start(f32[2,256,512]{2,1,0:T(8,128)S(1)} %get-tuple-element.12.strip_ref) | copy-start | bytes 3145732
  100.4 8.7 %collective-permute-start.14 = (f32[2,128,256]{2,1,0:T(8,128)S(1)}, f32[2,128,256]{2,1,0:T(8,128)S(1)}, u32[]{:S(2)}, u32[]{:S(2)}) collective-permute-start(f32[2,128,256]{2,1,0:T(8,128)S(1)} %get-tuple-element.15), channel_id=1, source_target_pairs={{0,2},{2,4},{4,6},{6,8},{8,10},{10,12},{12,14},{14,16},{16,18},{18... | collective-permute-start | bytes 786440 | tf_op jit(solution)/shard_map/ppermute | solution.py:383
  105.2 9.9 %collective-permute-start.15 = (f32[2,128,256]{2,1,0:T(8,128)S(1)}, f32[2,128,256]{2,1,0:T(8,128)S(1)}, u32[]{:S(2)}, u32[]{:S(2)}) collective-permute-start(f32[2,128,256]{2,1,0:T(8,128)S(1)} %get-tuple-element.16), channel_id=1, source_target_pairs={{2,0},{4,2},{6,4},{8,6},{10,8},{12,10},{14,12},{16,14},{18,16},{20... | collective-permute-start | bytes 786440 | tf_op jit(solution)/shard_map/ppermute | solution.py:386
  120.8 2.4 %collective-permute-start.21 = (f32[16,3,16,256]{3,2,1,0:T(8,128)S(1)}, f32[16,3,16,256]{3,2,1,0:T(8,128)S(1)}, u32[]{:S(2)}, u32[]{:S(2)}) collective-permute-start(f32[16,3,16,256]{3,2,1,0:T(8,128)S(1)} %get-tuple-element.19), channel_id=1, source_target_pairs={{0,1},{1,0},{2,3},{3,2},{4,5},{5,4},{6,7},{7,6},{8,9},{9,8},{10,11... | collective-permute-start | bytes 2359304 | tf_op jit(solution)/shard_map/ppermute | solution.py:377
  153.7 29.9 %all-to-all-start.3 = ((f32[16,2,16,256]{3,2,1,0:T(8,128)}), f32[16,2,16,256]{3,2,1,0:T(8,128)S(1)}, u32[]{:S(2)}, u32[]{:S(2)}) async-start(f32[16,2,16,256]{3,2,1,0:T(8,128)} %piece.3), calls=%async_computation.3 | async-start | bytes 1048576 | tf_op jit(solution)/shard_map/all_to_all | solution.py:380
  157.3 23.1 %collective-permute-start.16 = (f32[2,256,256]{2,1,0:T(8,128)S(1)}, f32[2,256,256]{2,1,0:T(8,128)S(1)}, u32[]{:S(2)}, u32[]{:S(2)}) collective-permute-start(f32[2,256,256]{2,1,0:T(8,128)S(1)} %get-tuple-element.17.own), channel_id=1, source_target_pairs={{0,1},{1,0},{2,3},{3,2},{4,5},{5,4},{6,7},{7,6},{8,9},{9,8},{10,11... | collective-permute-start | bytes 1572872 | tf_op jit(solution)/shard_map/ppermute | solution.py:377
  157.4 23.0 %copy-start.4 = (f32[2,256,512]{2,1,0:T(8,128)S(1)}, f32[2,256,512]{2,1,0:T(8,128)}, u32[]{:S(2)}) copy-start(f32[2,256,512]{2,1,0:T(8,128)} %copy-done.3) | copy-start | bytes 3145732
  157.4 18.9 %collective-permute-start.17 = (f32[2,128,256]{2,1,0:T(8,128)S(1)}, f32[2,128,256]{2,1,0:T(8,128)S(1)}, u32[]{:S(2)}, u32[]{:S(2)}) collective-permute-start(f32[2,128,256]{2,1,0:T(8,128)S(1)} %get-tuple-element.23), channel_id=1, source_target_pairs={{0,2},{2,4},{4,6},{6,8},{8,10},{10,12},{12,14},{14,16},{16,18},{18... | collective-permute-start | bytes 786440 | tf_op jit(solution)/shard_map/ppermute | solution.py:383
  161.2 17.0 %collective-permute-start.18 = (f32[2,128,256]{2,1,0:T(8,128)S(1)}, f32[2,128,256]{2,1,0:T(8,128)S(1)}, u32[]{:S(2)}, u32[]{:S(2)}) collective-permute-start(f32[2,128,256]{2,1,0:T(8,128)S(1)} %get-tuple-element.22), channel_id=1, source_target_pairs={{2,0},{4,2},{6,4},{8,6},{10,8},{12,10},{14,12},{16,14},{18,16},{20... | collective-permute-start | bytes 786440 | tf_op jit(solution)/shard_map/ppermute | solution.py:386
  176.3 4.1 %collective-permute-start.19 = (f32[2,128,256]{2,1,0:T(8,128)S(1)}, f32[2,128,256]{2,1,0:T(8,128)S(1)}, u32[]{:S(2)}, u32[]{:S(2)}) collective-permute-start(f32[2,128,256]{2,1,0:T(8,128)S(1)} %collective-permute-done.17.b0), channel_id=1, source_target_pairs={{0,1},{1,0},{2,3},{3,2},{4,5},{5,4},{6,7},{7,6},{8,9},{9,8},{10,11... | collective-permute-start | bytes 786440 | tf_op jit(solution)/shard_map/ppermute | solution.py:377
  178.2 2.2 %collective-permute-start.20 = (f32[2,128,256]{2,1,0:T(8,128)S(1)}, f32[2,128,256]{2,1,0:T(8,128)S(1)}, u32[]{:S(2)}, u32[]{:S(2)}) collective-permute-start(f32[2,128,256]{2,1,0:T(8,128)S(1)} %collective-permute-done.18.a0), channel_id=1, source_target_pairs={{0,1},{1,0},{2,3},{3,2},{4,5},{5,4},{6,7},{7,6},{8,9},{9,8},{10,11... | collective-permute-start | bytes 786440 | tf_op jit(solution)/shard_map/ppermute | solution.py:377
where the time goes:
time: 186 us; the launch traced here: 185 us
  waiting for transfers between devices  61.3 us (33%)
  blocking collectives  56.3 us (30%)
  starting transfers between devices  35.1 us (19%)
  Pallas kernels  25.2 us (14%)
  local copies, waits for them, and re-layouts  5.66 us (3%)
    all_to_all x2, blocking collectives, to_all(): return lax.all_to_all(blocks, 'tile', 0, 0, tiled=True)  56.3 us
    ppermute x5, waiting for transfers between devices, from_below(): return lax.ppermute(value, 'tile', up)  39.8 us
    pallas_call x9, Pallas kernels, call(): pl.pallas_call(kernel, out_shape=shapes, in_specs=[smem] + [pl.BlockSpec(...  25.2 us
    ppermute x5, starting transfers between devices, from_below(): return lax.ppermute(value, 'tile', up)  20.5 us
    ppermute x5, waiting for transfers between devices, from_above(): return lax.ppermute(value, 'tile', down)  16.5 us
    all_to_all x2, starting transfers between devices, to_all(): return lax.all_to_all(blocks, 'tile', 0, 0, tiled=True)  7.15 us
    ppermute x5, starting transfers between devices, from_above(): return lax.ppermute(value, 'tile', down)  6.45 us
    ppermute x12, waiting for transfers between devices, swap(): return lax.ppermute(value, 'mode', [(0, 1), (1, 0)])  5.11 us
  transfers between devices with their start and end apart: 24, of which 13 were waited for; matrix products, arithmetic and copies ran while one was open for 0% of the time, Pallas kernels for 5%

commit v1 on v0

--- a/solution.py
+++ b/solution.py
@@ -217,9 +217,26 @@
     out[...] = tall[kept]
 
 
-def field_kernel(size, minibatch, info, strip_ref, *refs):
-    edges, (own, other, measured, table) = refs[:-10], refs[-10:-6]
-    gradient, step_own, step_other, window, observed, arrived = refs[-6:]
+def patch_kernel(size, minibatch, info, strip_ref, *refs):
+    edges, (patch, coverage, window) = refs[:-3], refs[-3:]
+    tiles, strip, pattern = size
+
+    def edge(side, part):
+        if len(edges) == 2:
+            return edges[side][part]
+        return jnp.where(info[25] == part, edges[2 * side][...], edges[2 * side + 1][...])
+
+    for part in range(2):
+        value = cut_patch(
+            size, info, minibatch, strip_ref, edge(0, part), edge(1, part), window, part
+        )
+        patch[part] = value
+    power = patch[0] * patch[0] + patch[1] * patch[1]
+    coverage[...] = power.reshape(coverage.shape)
+
+
+def field_kernel(size, minibatch, info, patch, own, other, measured, table, *refs):
+    gradient, step_own, step_other, observed, arrived = refs
     tiles, strip, pattern = size
     slot = info[25]
     fetch = pltpu.make_async_copy(measured.at[minibatch, slot], observed, arrived)
@@ -243,15 +260,7 @@
         block(cos_high, -sin_high, sin_high, cos_high),
         block(cos_low, -sin_low, sin_low, cos_low),
     )
-    def edge(side, part):
-        if len(edges) == 2:
-            return edges[side][part]
-        return jnp.where(slot == part, edges[2 * side][...], edges[2 * side + 1][...])
-
-    obj_real, obj_imag = (
-        cut_patch(size, info, minibatch, strip_ref, edge(0, part), edge(1, part), window, part)
-        for part in range(2)
-    )
+    obj_real, obj_imag = patch[0], patch[1]
     probes = [(part_of(ref, 0), part_of(ref, 1)) for ref in (own, other)]
 
     def both(fields, left, right):
@@ -278,13 +287,11 @@
     (cr0, ci0), (cr1, ci1) = chi
     gradient[0] = (pr0 * cr0 + pi0 * ci0) + (pr1 * cr1 + pi1 * ci1)
     gradient[1] = (pr0 * ci0 - pi0 * cr0) + (pr1 * ci1 - pi1 * cr1)
-    coverage = obj_real * obj_real + obj_imag * obj_imag
     rows = pattern // tiles
     for step, (cr, ci) in ((step_own, chi[0]), (step_other, chi[1])):
         for part, value in (
             (0, obj_real * cr + obj_imag * ci),
             (1, obj_real * ci - obj_imag * cr),
-            (2, coverage),
         ):
             step[:, part] = value.reshape(tiles, rows, pattern)
 
@@ -317,13 +324,22 @@
             edges[1][part] = take_columns(fresh[strip - half :], column_above, pattern)
 
 
-def piece_kernel(info, sums, probe, out):
+def total_of(sums):
+    total = sums[0]
+    for k in range(1, sums.shape[0]):
+        total += sums[k]
+    return total
+
+
+def sum_kernel(info, sums, out):
+    out[...] = total_of(sums)
+
+
+def piece_kernel(info, sums, coverage, coverage_other, probe, out):
     tiles, parts, rows, width = sums.shape
     tile = info[24]
-    total = sums[0]
-    for k in range(1, tiles):
-        total += sums[k]
-    divisor = total[2] + 1.0
+    total = total_of(sums)
+    divisor = coverage[...] + coverage_other[...] + 1.0
     for part in range(2):
         if len(probe.shape) == 3:
             held = probe[part, pl.ds(pl.multiple_of(tile * rows, rows), rows), :]
@@ -392,22 +408,33 @@
     tile, slot = lax.axis_index("tile"), lax.axis_index("mode")
     one_part = lax.dynamic_index_in_dim(object_field, slot, 0, keepdims=False)
     edges = [from_below(one_part[strip - half :]), from_above(one_part[:half])]
+    below, above = from_below(positions), from_above(positions)
+    *edges, below, above = lax.optimization_barrier((*edges, below, above))
     edges = [edges[0], swap(edges[0]), edges[1], swap(edges[1])]
     index = jnp.stack([tile, slot]).astype(jnp.int32)
-    below, above = from_below(positions), from_above(positions)
     here = jnp.concatenate([positions.ravel()] * 3 + [index])
     info = jnp.concatenate([below.ravel(), positions.ravel(), above.ravel(), index])
     own = probe[0]
     other = swap(own)
 
     for minibatch in range(2):
-        blocks = (tiles, 3, pattern // tiles, pattern)
+        rows = pattern // tiles
+        patch, coverage = call(
+            bind(patch_kernel, size, minibatch),
+            "patch",
+            [field, (tiles, rows, pattern)],
+            (here, object_field, *edges),
+            [window],
+        )
+        (coverage,) = call(sum_kernel, "coverage", [(rows, pattern)], (here, to_all(coverage)))
+        coverage_other = swap(coverage)
+        blocks = (tiles, 2, rows, pattern)
         gradient, step_own, step_other = call(
             bind(field_kernel, size, minibatch),
             "field",
             [field, blocks, blocks],
-            (here, object_field, *edges, own, other, measured, table),
-            [window, (pattern, pattern)],
+            (here, patch, own, other, measured, table),
+            [(pattern, pattern)],
             flops=2 * 12 * 512**3,
             far=measured,
         )
@@ -419,6 +446,8 @@
             [tall],
         )
         rim_below, rim_above = from_below(gradient[:, half:]), from_above(gradient[:, :half])
+        sums = to_all(step_own + swap(step_other))
+        sums, rim_below, rim_above = lax.optimization_barrier((sums, rim_below, rim_above))
         rims = (gradient, swap(gradient), rim_below, rim_above, swap(rim_below), swap(rim_above))
         last = minibatch == 1
         object_field, *edges = call(
@@ -431,9 +460,8 @@
         if not last:
             edges = [from_below(edges[1]), from_above(edges[0])]
 
-        sums = to_all(step_own + swap(step_other))
         (fresh,) = call(
-            piece_kernel, "piece", [(tiles, 2, pattern // tiles, pattern)], (here, sums, own)
+            piece_kernel, "piece", [blocks], (here, sums, coverage, coverage_other, own)
         )
         own = to_all(fresh)
         if not last:

time: 186 us -> 186 us (level)
  blocking collectives: 56.3 us -> 0 us
  starting transfers between devices: 35.1 us -> 62.6 us
  waiting for transfers between devices: 61.3 us -> 85.9 us
  Pallas kernels: 25.2 us -> 29.8 us
  local copies, waits for them, and re-layouts: 5.66 us -> 1.68 us
  other arithmetic: 0.28 us -> 3.89 us
    all_to_all x2 -> x0, blocking collectives: 56.3 us -> none  [to_all(): return lax.all_to_all(blocks, 'tile', 0, 0, tiled=True)]
    all_to_all x2 -> x6, waiting for transfers between devices: 0.01 us -> 39.8 us  [to_all(): return lax.all_to_all(blocks, 'tile', 0, 0, tiled=True)]
    all_to_all x2 -> x6, starting transfers between devices: 7.15 us -> 32.6 us  [to_all(): return lax.all_to_all(blocks, 'tile', 0, 0, tiled=True)]
    ppermute x5, waiting for transfers between devices: 39.8 us -> 25.4 us  [from_below(): return lax.ppermute(value, 'tile', up)]
    pallas_call x9 -> x13, Pallas kernels: 25.2 us -> 29.8 us  [call(): pl.pallas_call(kernel, out_shape=shapes, in_specs=[smem] + [pl.BlockSpec(...]
    unnamed x20 -> x18, local copies, waits for them, and re-layouts: 4.02 us -> 0.04 us
    ppermute x12 -> x14, waiting for transfers between devices: 5.11 us -> 1.26 us  [swap(): return lax.ppermute(value, 'mode', [(0, 1), (1, 0)])]
    add x2, other arithmetic: 0.28 us -> 3.89 us  [shards_by_position(): sums = to_all(step_own + swap(step_other))]
  transfers between devices with their start and end apart: 24 -> 30, of which waited for: 13 -> 14; matrix products, arithmetic and copies ran while one was open for 0% -> 2% of each run, Pallas kernels for 5% -> 8%
where the time goes in v1:
time: 186 us; the launch traced here: 185 us
  waiting for transfers between devices  85.9 us (46%)
  starting transfers between devices  62.6 us (34%)
  Pallas kernels  29.8 us (16%)
  other arithmetic  3.89 us (2%)
    all_to_all x6, waiting for transfers between devices, to_all(): return lax.all_to_all(blocks, 'tile', 0, 0, tiled=True)  39.8 us
    all_to_all x6, starting transfers between devices, to_all(): return lax.all_to_all(blocks, 'tile', 0, 0, tiled=True)  32.6 us
    pallas_call x13, Pallas kernels, call(): pl.pallas_call(kernel, out_shape=shapes, in_specs=[smem] + [pl.BlockSpec(...  29.8 us
    ppermute x5, waiting for transfers between devices, from_below(): return lax.ppermute(value, 'tile', up)  25.4 us
    ppermute x5, starting transfers between devices, from_below(): return lax.ppermute(value, 'tile', up)  21.1 us
    ppermute x5, waiting for transfers between devices, from_above(): return lax.ppermute(value, 'tile', down)  19.5 us
    ppermute x5, starting transfers between devices, from_above(): return lax.ppermute(value, 'tile', down)  6.64 us
    add x2, other arithmetic, shards_by_position(): sums = to_all(step_own + swap(step_other))  3.89 us
  transfers between devices with their start and end apart: 30, of which 14 were waited for; matrix products, arithmetic and copies ran while one was open for 2% of the time, Pallas kernels for 8%

profile of v1, /device:TPU:0, one launch (start us, length us, event | category | flops | bytes accessed | tf_op | source)
XLA Modules:
  0.0 184.9 jit_solution(17464556854221593205)
XLA Ops:
  0.6 1.2 dynamic-slice_bitcast_fusion
  1.8 4.9 %collective-permute-start = (f32[128,512]{1,0:T(8,128)S(1)}, f32[128,512]{1,0:T(8,128)S(1)}, u32[]{:S(2)}, u32[]{:S(2)}) collective-permute-start(f32[128,512]{1,0:T(8,128)S(1)} %get-tuple-element.49), channel_id=1, source_target_pairs={{0,2},{2,4},{4,6},{6,8},{8,10},{10,12},{12,14},{14,16},{16,18},{18... | collective-permute-start | bytes 786440 | tf_op jit(solution)/shard_map/ppermute | solution.py:399
  6.7 1.3 collective-permute-start.1
  8.1 4.5 %collective-permute-start.2 = (s32[2,2,2]{2,1,0:T(2,128)S(1)}, s32[2,2,2]{2,1,0:T(2,128)S(1)}, u32[]{:S(2)}, u32[]{:S(2)}) collective-permute-start(s32[2,2,2]{2,1,0:T(2,128)S(1)} %copy-done.8), channel_id=1, source_target_pairs={{0,2},{2,4},{4,6},{6,8},{8,10},{10,12},{12,14},{14,16},{16,18},{18... | collective-permute-start | bytes 104 | tf_op jit(solution)/shard_map/ppermute | solution.py:399
  12.6 1.3 collective-permute-start.3
  13.9 4.0 %collective-permute-done.2 = s32[2,2,2]{2,1,0:T(2,128)S(1)} collective-permute-done((s32[2,2,2]{2,1,0:T(2,128)S(1)}, s32[2,2,2]{2,1,0:T(2,128)S(1)}, u32[]{:S(2)}, u32[]{:S(2)}) %collective-permute-start.2) | collective-permute-done | bytes 64 | tf_op jit(solution)/shard_map/ppermute | solution.py:399
  17.9 2.0 %collective-permute-done.3 = s32[2,2,2]{2,1,0:T(2,128)S(1)} collective-permute-done((s32[2,2,2]{2,1,0:T(2,128)S(1)}, s32[2,2,2]{2,1,0:T(2,128)S(1)}, u32[]{:S(2)}, u32[]{:S(2)}) %collective-permute-start.3) | collective-permute-done | bytes 64 | tf_op jit(solution)/shard_map/ppermute | solution.py:402
  19.9 0.5 collective-permute-start.6
  20.6 0.9 collective-permute-done.5.refs_1_
  21.8 2.0 %patch.2 = (f32[2,256,256]{2,1,0:T(8,128)S(1)}, f32[16,16,256]{2,1,0:T(8,128)}) custom-call(s32[26]{0:T(128)S(1)} %concatenate.9.info, f32[2,256,512]{2,1,0:T(8,128)S(1)} %copy-done, f32[128,512]{1,0:T(8,128)S(1)} %collective-permute-done.refs_0_, f32[128,512]{1,0:T(8,128)S(1)} %collective-permute-done.5.refs_1_, ...), custom_call_target="tpu_custom_call" | custom-call | bytes 2883688 | tf_op jit(solution)/shard_map/patch/pallas_call | solution.py:365
  23.9 5.3 %field.2 = (f32[2,256,256]{2,1,0:T(8,128)S(1)}, f32[16,2,16,256]{3,2,1,0:T(8,128)S(1)}, f32[16,2,16,256]{3,2,1,0:T(8,128)}) custom-call(s32[26]{0:T(128)S(1)} %concatenate.9.info, f32[2,256,256]{2,1,0:T(8,128)S(1)} %get-tuple-element.29.patch, f32[2,256,256]{2,1,0:T(8,128)S(1)} %bitcast.9, f32[2,256,256]{2,1,0:T(8,128)S(1)} %collective-permute-done.4.other, ...), custom_call_target="tpu_custom_call" | custom-call | flops 3221225472 | bytes 4718696 | tf_op jit(solution)/shard_map/field/pallas_call | solution.py:365
  29.4 7.7 %all-to-all-start.1 = ((f32[16,16,256]{2,1,0:T(8,128)}), f32[16,16,256]{2,1,0:T(8,128)S(1)}, u32[]{:S(2)}, u32[]{:S(2)}) async-start(f32[16,16,256]{2,1,0:T(8,128)} %get-tuple-element.37), calls=%async_computation.1 | async-start | bytes 524288 | tf_op jit(solution)/shard_map/all_to_all | solution.py:396
  37.1 1.9 %add.11 = f32[16,2,16,256]{3,2,1,0:T(8,128)} add(f32[16,2,16,256]{3,2,1,0:T(8,128)S(1)} %get-tuple-element.31, f32[16,2,16,256]{3,2,1,0:T(8,128)} %collective-permute-done.8) | non-fusion elementwise | flops 131072 | bytes 1572864 | tf_op jit(solution)/shard_map/add | solution.py:449
  39.1 8.4 %all-to-all-done.1.sums = f32[16,16,256]{2,1,0:T(8,128)S(1)} async-done(((f32[16,16,256]{2,1,0:T(8,128)}), f32[16,16,256]{2,1,0:T(8,128)S(1)}, u32[]{:S(2)}, u32[]{:S(2)}) %all-to-all-start.1) | async-done | bytes 262176 | tf_op jit(solution)/shard_map/all_to_all | solution.py:396
  47.5 3.6 %all-to-all-start = ((f32[16,2,16,256]{3,2,1,0:T(8,128)}), f32[16,2,16,256]{3,2,1,0:T(8,128)S(1)}, u32[]{:S(2)}, u32[]{:S(2)}) async-start(f32[16,2,16,256]{3,2,1,0:T(8,128)} %add.11), calls=%async_computation | async-start | bytes 1048576 | tf_op jit(solution)/shard_map/all_to_all | solution.py:396
  51.2 1.3 collective-permute-start.10
  52.5 5.3 %collective-permute-start.9 = (f32[2,128,256]{2,1,0:T(8,128)S(1)}, f32[2,128,256]{2,1,0:T(8,128)}, u32[]{:S(2)}, u32[]{:S(2)}) collective-permute-start(f32[2,128,256]{2,1,0:T(8,128)S(1)} %get-tuple-element.53), channel_id=1, source_target_pairs={{0,2},{2,4},{4,6},{6,8},{8,10},{10,12},{12,14},{14,16},{16,18},{18... | collective-permute-start | bytes 786440 | tf_op jit(solution)/shard_map/ppermute | solution.py:399
  57.7 0.6 coverage.2
  58.4 7.6 %collective-permute-done.10.a0 = f32[2,128,256]{2,1,0:T(8,128)S(1)} collective-permute-done((f32[2,128,256]{2,1,0:T(8,128)S(1)}, f32[2,128,256]{2,1,0:T(8,128)S(1)}, u32[]{:S(2)}, u32[]{:S(2)}) %collective-permute-start.10) | collective-permute-done | bytes 262176 | tf_op jit(solution)/shard_map/ppermute | solution.py:402
  65.9 4.7 %collective-permute-done.9.b0 = f32[2,128,256]{2,1,0:T(8,128)} collective-permute-done((f32[2,128,256]{2,1,0:T(8,128)S(1)}, f32[2,128,256]{2,1,0:T(8,128)}, u32[]{:S(2)}, u32[]{:S(2)}) %collective-permute-start.9) | collective-permute-done | bytes 262176 | tf_op jit(solution)/shard_map/ppermute | solution.py:399
  70.6 1.4 piece.2
  72.0 6.8 %all-to-all-start.2 = ((f32[16,2,16,256]{3,2,1,0:T(8,128)}), f32[16,2,16,256]{3,2,1,0:T(8,128)S(1)}, u32[]{:S(2)}, u32[]{:S(2)}) async-start(f32[16,2,16,256]{3,2,1,0:T(8,128)} %piece.2), calls=%async_computation.2 | async-start | bytes 1048576 | tf_op jit(solution)/shard_map/all_to_all | solution.py:396
  78.9 0.5 collective-permute-start.11
  79.5 14.2 %all-to-all-done.2.own.probe = f32[16,2,16,256]{3,2,1,0:T(8,128)S(1)} async-done(((f32[16,2,16,256]{3,2,1,0:T(8,128)}), f32[16,2,16,256]{3,2,1,0:T(8,128)S(1)}, u32[]{:S(2)}, u32[]{:S(2)}) %all-to-all-start.2) | async-done | bytes 524320 | tf_op jit(solution)/shard_map/all_to_all | solution.py:396
  93.9 1.7 illumination.2.illum
  95.7 3.2 %update.2 = (f32[2,256,512]{2,1,0:T(8,128)S(1)}, f32[2,128,256]{2,1,0:T(8,128)S(1)}, f32[2,128,256]{2,1,0:T(8,128)S(1)}) custom-call(s32[26]{0:T(128)S(1)} %concatenate.8.info, f32[2,256,512]{2,1,0:T(8,128)S(1)} %copy-done, f32[256,512]{1,0:T(8,128)S(1)} %illumination.2.illum, f32[2,256,256]{2,1,0:T(8,128)S(1)} %get-tuple-element.30.own, ...), custom_call_target="tpu_custom_call" | custom-call | bytes 5242984 | tf_op jit(solution)/shard_map/update/pallas_call | solution.py:365
  98.9 2.6 %collective-permute-start.15 = (f32[2,128,256]{2,1,0:T(8,128)S(1)}, f32[2,128,256]{2,1,0:T(8,128)S(1)}, u32[]{:S(2)}, u32[]{:S(2)}) collective-permute-start(f32[2,128,256]{2,1,0:T(8,128)S(1)} %get-tuple-element.38), channel_id=1, source_target_pairs={{0,2},{2,4},{4,6},{6,8},{8,10},{10,12},{12,14},{14,16},{16,18},{18... | collective-permute-start | bytes 786440 | tf_op jit(solution)/shard_map/ppermute | solution.py:399
  101.5 1.5 collective-permute-start.16
  103.0 4.7 %collective-permute-done.15.refs_0_ = f32[2,128,256]{2,1,0:T(8,128)S(1)} collective-permute-done((f32[2,128,256]{2,1,0:T(8,128)S(1)}, f32[2,128,256]{2,1,0:T(8,128)S(1)}, u32[]{:S(2)}, u32[]{:S(2)}) %collective-permute-start.15) | collective-permute-done | bytes 262176 | tf_op jit(solution)/shard_map/ppermute | solution.py:399
  107.7 7.9 %collective-permute-done.16.refs_1_ = f32[2,128,256]{2,1,0:T(8,128)S(1)} collective-permute-done((f32[2,128,256]{2,1,0:T(8,128)S(1)}, f32[2,128,256]{2,1,0:T(8,128)S(1)}, u32[]{:S(2)}, u32[]{:S(2)}) %collective-permute-start.16) | collective-permute-done | bytes 262176 | tf_op jit(solution)/shard_map/ppermute | solution.py:402
  115.6 1.7 patch.3
  117.3 5.1 %field.3 = (f32[2,256,256]{2,1,0:T(8,128)S(1)}, f32[16,2,16,256]{3,2,1,0:T(8,128)S(1)}, f32[16,2,16,256]{3,2,1,0:T(8,128)S(1)}) custom-call(s32[26]{0:T(128)S(1)} %concatenate.9.info, f32[2,256,256]{2,1,0:T(8,128)S(1)} %get-tuple-element.40.patch, f32[16,2,16,256]{3,2,1,0:T(8,128)S(1)} %all-to-all-done.2.own.probe, ...), custom_call_target="tpu_custom_call" | custom-call | flops 3221225472 | bytes 4718696 | tf_op jit(solution)/shard_map/field/pallas_call | solution.py:365
  122.5 4.5 %all-to-all-start.4 = ((f32[16,16,256]{2,1,0:T(8,128)}), f32[16,16,256]{2,1,0:T(8,128)S(1)}, u32[]{:S(2)}, u32[]{:S(2)}) async-start(f32[16,16,256]{2,1,0:T(8,128)} %get-tuple-element.47), calls=%async_computation.4 | async-start | bytes 524288 | tf_op jit(solution)/shard_map/all_to_all | solution.py:396
  127.0 2.0 %add.12 = f32[16,2,16,256]{3,2,1,0:T(8,128)} add(f32[16,2,16,256]{3,2,1,0:T(8,128)S(1)} %get-tuple-element.42, f32[16,2,16,256]{3,2,1,0:T(8,128)} %collective-permute-done.18) | non-fusion elementwise | flops 131072 | bytes 1572864 | tf_op jit(solution)/shard_map/add | solution.py:449
  128.9 8.5 %all-to-all-done.4.sums = f32[16,16,256]{2,1,0:T(8,128)S(1)} async-done(((f32[16,16,256]{2,1,0:T(8,128)}), f32[16,16,256]{2,1,0:T(8,128)S(1)}, u32[]{:S(2)}, u32[]{:S(2)}) %all-to-all-start.4) | async-done | bytes 262176 | tf_op jit(solution)/shard_map/all_to_all | solution.py:396
  137.5 3.6 %all-to-all-start.3 = ((f32[16,2,16,256]{3,2,1,0:T(8,128)}), f32[16,2,16,256]{3,2,1,0:T(8,128)S(1)}, u32[]{:S(2)}, u32[]{:S(2)}) async-start(f32[16,2,16,256]{3,2,1,0:T(8,128)} %add.12), calls=%async_computation.3 | async-start | bytes 1048576 | tf_op jit(solution)/shard_map/all_to_all | solution.py:396
  141.1 3.8 %collective-permute-start.19 = (f32[2,128,256]{2,1,0:T(8,128)S(1)}, f32[2,128,256]{2,1,0:T(8,128)S(1)}, u32[]{:S(2)}, u32[]{:S(2)}) collective-permute-start(f32[2,128,256]{2,1,0:T(8,128)S(1)} %get-tuple-element.51), channel_id=1, source_target_pairs={{0,2},{2,4},{4,6},{6,8},{8,10},{10,12},{12,14},{14,16},{16,18},{18... | collective-permute-start | bytes 786440 | tf_op jit(solution)/shard_map/ppermute | solution.py:399
  144.9 1.3 collective-permute-start.20
  146.2 0.6 coverage.3
  146.9 12.0 %collective-permute-done.19.b0 = f32[2,128,256]{2,1,0:T(8,128)S(1)} collective-permute-done((f32[2,128,256]{2,1,0:T(8,128)S(1)}, f32[2,128,256]{2,1,0:T(8,128)S(1)}, u32[]{:S(2)}, u32[]{:S(2)}) %collective-permute-start.19) | collective-permute-done | bytes 262176 | tf_op jit(solution)/shard_map/ppermute | solution.py:399
  158.9 2.1 %collective-permute-done.20.a0 = f32[2,128,256]{2,1,0:T(8,128)S(1)} collective-permute-done((f32[2,128,256]{2,1,0:T(8,128)S(1)}, f32[2,128,256]{2,1,0:T(8,128)S(1)}, u32[]{:S(2)}, u32[]{:S(2)}) %collective-permute-start.20) | collective-permute-done | bytes 262176 | tf_op jit(solution)/shard_map/ppermute | solution.py:402
  161.0 1.4 piece.3
  162.4 6.4 %all-to-all-start.5 = ((f32[16,2,16,256]{3,2,1,0:T(8,128)}), f32[16,2,16,256]{3,2,1,0:T(8,128)S(1)}, u32[]{:S(2)}, u32[]{:S(2)}) async-start(f32[16,2,16,256]{3,2,1,0:T(8,128)} %piece.3), calls=%async_computation.5 | async-start | bytes 1048576 | tf_op jit(solution)/shard_map/all_to_all | solution.py:396
  168.9 0.5 collective-permute-start.21
  169.5 2.3 %illumination.3.illum = f32[256,512]{1,0:T(8,128)S(1)} custom-call(s32[26]{0:T(128)S(1)} %concatenate.8.info, f32[16,2,16,256]{3,2,1,0:T(8,128)S(1)} %all-to-all-done.2.own.probe, f32[16,2,16,256]{3,2,1,0:T(8,128)} %collective-permute-done.14.other), custom_call_target="tpu_custom_call" | custom-call | bytes 1572968 | tf_op jit(solution)/shard_map/illumination/pallas_call | solution.py:365
  171.8 3.2 %update.3 = f32[2,256,512]{2,1,0:T(8,128)} custom-call(s32[26]{0:T(128)S(1)} %concatenate.8.info, f32[2,256,512]{2,1,0:T(8,128)S(1)} %get-tuple-element.35.strip_ref, f32[256,512]{1,0:T(8,128)S(1)} %illumination.3.illum, f32[2,256,256]{2,1,0:T(8,128)S(1)} %get-tuple-element.41.own, f32[2,256,256]{2,1,0:T(8,128)S(1)} %collective-permute-done.17.other, ...), custom_call_target="tpu_custom_call" | custom-call | bytes 4718696 | tf_op jit(solution)/shard_map/update/pallas_call | solution.py:365
  175.0 8.6 %all-to-all-done.5.blocks = f32[16,2,16,256]{3,2,1,0:T(8,128)S(1)} async-done(((f32[16,2,16,256]{3,2,1,0:T(8,128)}), f32[16,2,16,256]{3,2,1,0:T(8,128)S(1)}, u32[]{:S(2)}, u32[]{:S(2)}) %all-to-all-start.5) | async-done | bytes 524320 | tf_op jit(solution)/shard_map/all_to_all | solution.py:396
  183.6 1.4 gather.1
  (53 shorter events, 1.8 us)
Async XLA Ops:
  0.6 21.2 %copy-start = (f32[2,256,512]{2,1,0:T(8,128)S(1)}, f32[2,256,512]{2,1,0:T(8,128)}, u32[]{:S(2)}) copy-start(f32[2,256,512]{2,1,0:T(8,128)} %strip_ref.3) | copy-start | bytes 3145732
  1.8 6.3 %copy-start.8 = (s32[2,2,2]{2,1,0:T(2,128)S(1)}, s32[2,2,2]{2,1,0:T(2,128)}, u32[]{:S(2)}) copy-start(s32[2,2,2]{2,1,0:T(2,128)} %param.7) | copy-start | bytes 100
  1.8 18.1 %collective-permute-start = (f32[128,512]{1,0:T(8,128)S(1)}, f32[128,512]{1,0:T(8,128)S(1)}, u32[]{:S(2)}, u32[]{:S(2)}) collective-permute-start(f32[128,512]{1,0:T(8,128)S(1)} %get-tuple-element.49), channel_id=1, source_target_pairs={{0,2},{2,4},{4,6},{6,8},{8,10},{10,12},{12,14},{14,16},{16,18},{18... | collective-permute-start | bytes 786440 | tf_op jit(solution)/shard_map/ppermute | solution.py:399
  6.7 13.2 %collective-permute-start.1 = (f32[128,512]{1,0:T(8,128)S(1)}, f32[128,512]{1,0:T(8,128)S(1)}, u32[]{:S(2)}, u32[]{:S(2)}) collective-permute-start(f32[128,512]{1,0:T(8,128)S(1)} %get-tuple-element.48), channel_id=1, source_target_pairs={{2,0},{4,2},{6,4},{8,6},{10,8},{12,10},{14,12},{16,14},{18,16},{20... | collective-permute-start | bytes 786440 | tf_op jit(solution)/shard_map/ppermute | solution.py:402
  8.0 15.8 %collective-permute-start.4 = (f32[2,256,256]{2,1,0:T(8,128)}, f32[2,256,256]{2,1,0:T(8,128)S(1)}, u32[]{:S(2)}, u32[]{:S(2)}) collective-permute-start(f32[2,256,256]{2,1,0:T(8,128)} %bitcast.8), channel_id=1, source_target_pairs={{0,1},{1,0},{2,3},{3,2},{4,5},{5,4},{6,7},{7,6},{8,9},{9,8},{10,11... | collective-permute-start | bytes 1572872 | tf_op jit(solution)/shard_map/ppermute | solution.py:393
  8.1 9.8 %collective-permute-start.2 = (s32[2,2,2]{2,1,0:T(2,128)S(1)}, s32[2,2,2]{2,1,0:T(2,128)S(1)}, u32[]{:S(2)}, u32[]{:S(2)}) collective-permute-start(s32[2,2,2]{2,1,0:T(2,128)S(1)} %copy-done.8), channel_id=1, source_target_pairs={{0,2},{2,4},{4,6},{6,8},{8,10},{10,12},{12,14},{14,16},{16,18},{18... | collective-permute-start | bytes 104 | tf_op jit(solution)/shard_map/ppermute | solution.py:399
  12.6 7.2 %collective-permute-start.3 = (s32[2,2,2]{2,1,0:T(2,128)S(1)}, s32[2,2,2]{2,1,0:T(2,128)S(1)}, u32[]{:S(2)}, u32[]{:S(2)}) collective-permute-start(s32[2,2,2]{2,1,0:T(2,128)S(1)} %copy-done.8), channel_id=1, source_target_pairs={{2,0},{4,2},{6,4},{8,6},{10,8},{12,10},{14,12},{16,14},{18,16},{20... | collective-permute-start | bytes 104 | tf_op jit(solution)/shard_map/ppermute | solution.py:402
  19.9 1.5 collective-permute-start.5
  19.9 1.9 %collective-permute-start.6 = (f32[128,512]{1,0:T(8,128)S(1)}, f32[128,512]{1,0:T(8,128)S(1)}, u32[]{:S(2)}, u32[]{:S(2)}) collective-permute-start(f32[128,512]{1,0:T(8,128)S(1)} %collective-permute-done.1.refs_2_), channel_id=1, source_target_pairs={{0,1},{1,0},{2,3},{3,2},{4,5},{5,4},{6,7},{7,6},{8,9},{9,8},{10,11... | collective-permute-start | bytes 786440 | tf_op jit(solution)/shard_map/ppermute | solution.py:393
  20.6 3.3 %copy-start.1 = (f32[1,2,256,256]{3,2,1,0:T(8,128)S(1)}, f32[1,2,256,256]{3,2,1,0:T(8,128)}, u32[]{:S(2)}) copy-start(f32[1,2,256,256]{3,2,1,0:T(8,128)} %param.6) | copy-start | bytes 1572868
  20.6 3.3 %copy-start.4 = (f32[2,2,256,256]{3,2,1,0:T(8,128)S(1)}, f32[2,2,256,256]{3,2,1,0:T(8,128)}, u32[]{:S(2)}) copy-start(f32[2,2,256,256]{3,2,1,0:T(8,128)} %measured.3) | copy-start | bytes 3145732
  20.6 3.3 %copy-start.6 = (f32[2,256,256]{2,1,0:T(8,128)S(1)}, f32[2,256,256]{2,1,0:T(8,128)}, u32[]{:S(2)}) copy-start(f32[2,256,256]{2,1,0:T(8,128)} %constant.16.clone.table) | copy-start | bytes 1572868
  23.8 5.4 %copy-start.2 = (f32[2,256,256]{2,1,0:T(8,128)}, f32[2,256,256]{2,1,0:T(8,128)S(1)}, u32[]{:S(2)}) copy-start(f32[2,256,256]{2,1,0:T(8,128)S(1)} %collective-permute-done.4.other) | copy-start | bytes 1572868
  29.2 7.9 %collective-permute-start.8 = (f32[16,2,16,256]{3,2,1,0:T(8,128)}, f32[16,2,16,256]{3,2,1,0:T(8,128)}, u32[]{:S(2)}, u32[]{:S(2)}) collective-permute-start(f32[16,2,16,256]{3,2,1,0:T(8,128)} %get-tuple-element.32), channel_id=1, source_target_pairs={{0,1},{1,0},{2,3},{3,2},{4,5},{5,4},{6,7},{7,6},{8,9},{9,8},{10,11... | collective-permute-start | bytes 1572872 | tf_op jit(solution)/shard_map/ppermute | solution.py:393
  29.4 18.1 %all-to-all-start.1 = ((f32[16,16,256]{2,1,0:T(8,128)}), f32[16,16,256]{2,1,0:T(8,128)S(1)}, u32[]{:S(2)}, u32[]{:S(2)}) async-start(f32[16,16,256]{2,1,0:T(8,128)} %get-tuple-element.37), calls=%async_computation.1 | async-start | bytes 524288 | tf_op jit(solution)/shard_map/all_to_all | solution.py:396
  47.5 23.1 %all-to-all-start = ((f32[16,2,16,256]{3,2,1,0:T(8,128)}), f32[16,2,16,256]{3,2,1,0:T(8,128)S(1)}, u32[]{:S(2)}, u32[]{:S(2)}) async-start(f32[16,2,16,256]{3,2,1,0:T(8,128)} %add.11), calls=%async_computation | async-start | bytes 1048576 | tf_op jit(solution)/shard_map/all_to_all | solution.py:396
  51.2 14.8 %collective-permute-start.10 = (f32[2,128,256]{2,1,0:T(8,128)S(1)}, f32[2,128,256]{2,1,0:T(8,128)S(1)}, u32[]{:S(2)}, u32[]{:S(2)}) collective-permute-start(f32[2,128,256]{2,1,0:T(8,128)S(1)} %get-tuple-element.52), channel_id=1, source_target_pairs={{2,0},{4,2},{6,4},{8,6},{10,8},{12,10},{14,12},{16,14},{18,16},{20... | collective-permute-start | bytes 786440 | tf_op jit(solution)/shard_map/ppermute | solution.py:402
  52.5 18.1 %collective-permute-start.9 = (f32[2,128,256]{2,1,0:T(8,128)S(1)}, f32[2,128,256]{2,1,0:T(8,128)}, u32[]{:S(2)}, u32[]{:S(2)}) collective-permute-start(f32[2,128,256]{2,1,0:T(8,128)S(1)} %get-tuple-element.53), channel_id=1, source_target_pairs={{0,2},{2,4},{4,6},{6,8},{8,10},{10,12},{12,14},{14,16},{16,18},{18... | collective-permute-start | bytes 786440 | tf_op jit(solution)/shard_map/ppermute | solution.py:399
  58.3 12.3 %collective-permute-start.13 = (f32[16,256]{1,0:T(8,128)S(1)}, f32[16,256]{1,0:T(8,128)S(1)}, u32[]{:S(2)}, u32[]{:S(2)}) collective-permute-start(f32[16,256]{1,0:T(8,128)S(1)} %coverage.2), channel_id=1, source_target_pairs={{0,1},{1,0},{2,3},{3,2},{4,5},{5,4},{6,7},{7,6},{8,9},{9,8},{10,11... | collective-permute-start | bytes 49160 | tf_op jit(solution)/shard_map/ppermute | solution.py:393
  72.0 21.9 %copy-start.3 = (f32[2,256,256]{2,1,0:T(8,128)S(1)}, f32[2,256,256]{2,1,0:T(8,128)}, u32[]{:S(2)}) copy-start(f32[2,256,256]{2,1,0:T(8,128)} %copy-done.2) | copy-start | bytes 1572868
  72.0 21.6 %all-to-all-start.2 = ((f32[16,2,16,256]{3,2,1,0:T(8,128)}), f32[16,2,16,256]{3,2,1,0:T(8,128)S(1)}, u32[]{:S(2)}, u32[]{:S(2)}) async-start(f32[16,2,16,256]{3,2,1,0:T(8,128)} %piece.2), calls=%async_computation.2 | async-start | bytes 1048576 | tf_op jit(solution)/shard_map/all_to_all | solution.py:396
  78.8 16.8 %collective-permute-start.7 = (f32[2,256,256]{2,1,0:T(8,128)S(1)}, f32[2,256,256]{2,1,0:T(8,128)}, u32[]{:S(2)}, u32[]{:S(2)}) collective-permute-start(f32[2,256,256]{2,1,0:T(8,128)S(1)} %get-tuple-element.30.own), channel_id=1, source_target_pairs={{0,1},{1,0},{2,3},{3,2},{4,5},{5,4},{6,7},{7,6},{8,9},{9,8},{10,11... | collective-permute-start | bytes 1572872 | tf_op jit(solution)/shard_map/ppermute | solution.py:393
  78.9 16.7 %collective-permute-start.11 = (f32[2,128,256]{2,1,0:T(8,128)}, f32[2,128,256]{2,1,0:T(8,128)}, u32[]{:S(2)}, u32[]{:S(2)}) collective-permute-start(f32[2,128,256]{2,1,0:T(8,128)} %collective-permute-done.9.b0), channel_id=1, source_target_pairs={{0,1},{1,0},{2,3},{3,2},{4,5},{5,4},{6,7},{7,6},{8,9},{9,8},{10,11... | collective-permute-start | bytes 786440 | tf_op jit(solution)/shard_map/ppermute | solution.py:393
  79.4 16.3 %collective-permute-start.12 = (f32[2,128,256]{2,1,0:T(8,128)S(1)}, f32[2,128,256]{2,1,0:T(8,128)}, u32[]{:S(2)}, u32[]{:S(2)}) collective-permute-start(f32[2,128,256]{2,1,0:T(8,128)S(1)} %collective-permute-done.10.a0), channel_id=1, source_target_pairs={{0,1},{1,0},{2,3},{3,2},{4,5},{5,4},{6,7},{7,6},{8,9},{9,8},{10,11... | collective-permute-start | bytes 786440 | tf_op jit(solution)/shard_map/ppermute | solution.py:393
  93.7 23.7 %collective-permute-start.14 = (f32[16,2,16,256]{3,2,1,0:T(8,128)S(1)}, f32[16,2,16,256]{3,2,1,0:T(8,128)}, u32[]{:S(2)}, u32[]{:S(2)}) collective-permute-start(f32[16,2,16,256]{3,2,1,0:T(8,128)S(1)} %all-to-all-done.2.own.probe), channel_id=1, source_target_pairs={{0,1},{1,0},{2,3},{3,2},{4,5},{5,4},{6,7},{7,6},{8,9},{9,8},{10,11... | collective-permute-start | bytes 1572872 | tf_op jit(solution)/shard_map/ppermute | solution.py:393
  98.9 18.4 %copy-start.5 = (f32[2,2,256,256]{3,2,1,0:T(8,128)S(1)}, f32[2,2,256,256]{3,2,1,0:T(8,128)}, u32[]{:S(2)}) copy-start(f32[2,2,256,256]{3,2,1,0:T(8,128)} %measured.3) | copy-start | bytes 3145732
  98.9 8.8 %collective-permute-start.15 = (f32[2,128,256]{2,1,0:T(8,128)S(1)}, f32[2,128,256]{2,1,0:T(8,128)S(1)}, u32[]{:S(2)}, u32[]{:S(2)}) collective-permute-start(f32[2,128,256]{2,1,0:T(8,128)S(1)} %get-tuple-element.38), channel_id=1, source_target_pairs={{0,2},{2,4},{4,6},{6,8},{8,10},{10,12},{12,14},{14,16},{16,18},{18... | collective-permute-start | bytes 786440 | tf_op jit(solution)/shard_map/ppermute | solution.py:399
  101.5 14.1 %collective-permute-start.16 = (f32[2,128,256]{2,1,0:T(8,128)S(1)}, f32[2,128,256]{2,1,0:T(8,128)S(1)}, u32[]{:S(2)}, u32[]{:S(2)}) collective-permute-start(f32[2,128,256]{2,1,0:T(8,128)S(1)} %get-tuple-element.39), channel_id=1, source_target_pairs={{2,0},{4,2},{6,4},{8,6},{10,8},{12,10},{14,12},{16,14},{18,16},{20... | collective-permute-start | bytes 786440 | tf_op jit(solution)/shard_map/ppermute | solution.py:402
  115.6 1.7 copy-start.7
  122.4 4.6 %collective-permute-start.18 = (f32[16,2,16,256]{3,2,1,0:T(8,128)S(1)}, f32[16,2,16,256]{3,2,1,0:T(8,128)}, u32[]{:S(2)}, u32[]{:S(2)}) collective-permute-start(f32[16,2,16,256]{3,2,1,0:T(8,128)S(1)} %get-tuple-element.43), channel_id=1, source_target_pairs={{0,1},{1,0},{2,3},{3,2},{4,5},{5,4},{6,7},{7,6},{8,9},{9,8},{10,11... | collective-permute-start | bytes 1572872 | tf_op jit(solution)/shard_map/ppermute | solution.py:393
  122.5 15.0 %all-to-all-start.4 = ((f32[16,16,256]{2,1,0:T(8,128)}), f32[16,16,256]{2,1,0:T(8,128)S(1)}, u32[]{:S(2)}, u32[]{:S(2)}) async-start(f32[16,16,256]{2,1,0:T(8,128)} %get-tuple-element.47), calls=%async_computation.4 | async-start | bytes 524288 | tf_op jit(solution)/shard_map/all_to_all | solution.py:396
  137.5 23.5 %all-to-all-start.3 = ((f32[16,2,16,256]{3,2,1,0:T(8,128)}), f32[16,2,16,256]{3,2,1,0:T(8,128)S(1)}, u32[]{:S(2)}, u32[]{:S(2)}) async-start(f32[16,2,16,256]{3,2,1,0:T(8,128)} %add.12), calls=%async_computation.3 | async-start | bytes 1048576 | tf_op jit(solution)/shard_map/all_to_all | solution.py:396
  141.1 17.8 %collective-permute-start.19 = (f32[2,128,256]{2,1,0:T(8,128)S(1)}, f32[2,128,256]{2,1,0:T(8,128)S(1)}, u32[]{:S(2)}, u32[]{:S(2)}) collective-permute-start(f32[2,128,256]{2,1,0:T(8,128)S(1)} %get-tuple-element.51), channel_id=1, source_target_pairs={{0,2},{2,4},{4,6},{6,8},{8,10},{10,12},{12,14},{14,16},{16,18},{18... | collective-permute-start | bytes 786440 | tf_op jit(solution)/shard_map/ppermute | solution.py:399
  144.9 16.1 %collective-permute-start.20 = (f32[2,128,256]{2,1,0:T(8,128)S(1)}, f32[2,128,256]{2,1,0:T(8,128)S(1)}, u32[]{:S(2)}, u32[]{:S(2)}) collective-permute-start(f32[2,128,256]{2,1,0:T(8,128)S(1)} %get-tuple-element.50), channel_id=1, source_target_pairs={{2,0},{4,2},{6,4},{8,6},{10,8},{12,10},{14,12},{16,14},{18,16},{20... | collective-permute-start | bytes 786440 | tf_op jit(solution)/shard_map/ppermute | solution.py:402
  146.8 14.2 %collective-permute-start.23 = (f32[16,256]{1,0:T(8,128)S(1)}, f32[16,256]{1,0:T(8,128)S(1)}, u32[]{:S(2)}, u32[]{:S(2)}) collective-permute-start(f32[16,256]{1,0:T(8,128)S(1)} %coverage.3), channel_id=1, source_target_pairs={{0,1},{1,0},{2,3},{3,2},{4,5},{5,4},{6,7},{7,6},{8,9},{9,8},{10,11... | collective-permute-start | bytes 49160 | tf_op jit(solution)/shard_map/ppermute | solution.py:393
  162.4 21.2 %all-to-all-start.5 = ((f32[16,2,16,256]{3,2,1,0:T(8,128)}), f32[16,2,16,256]{3,2,1,0:T(8,128)S(1)}, u32[]{:S(2)}, u32[]{:S(2)}) async-start(f32[16,2,16,256]{3,2,1,0:T(8,128)} %piece.3), calls=%async_computation.5 | async-start | bytes 1048576 | tf_op jit(solution)/shard_map/all_to_all | solution.py:396
  168.8 2.9 %collective-permute-start.17 = (f32[2,256,256]{2,1,0:T(8,128)S(1)}, f32[2,256,256]{2,1,0:T(8,128)S(1)}, u32[]{:S(2)}, u32[]{:S(2)}) collective-permute-start(f32[2,256,256]{2,1,0:T(8,128)S(1)} %get-tuple-element.41.own), channel_id=1, source_target_pairs={{0,1},{1,0},{2,3},{3,2},{4,5},{5,4},{6,7},{7,6},{8,9},{9,8},{10,11... | collective-permute-start | bytes 1572872 | tf_op jit(solution)/shard_map/ppermute | solution.py:393
  168.9 2.8 %collective-permute-start.21 = (f32[2,128,256]{2,1,0:T(8,128)S(1)}, f32[2,128,256]{2,1,0:T(8,128)S(1)}, u32[]{:S(2)}, u32[]{:S(2)}) collective-permute-start(f32[2,128,256]{2,1,0:T(8,128)S(1)} %collective-permute-done.19.b0), channel_id=1, source_target_pairs={{0,1},{1,0},{2,3},{3,2},{4,5},{5,4},{6,7},{7,6},{8,9},{9,8},{10,11... | collective-permute-start | bytes 786440 | tf_op jit(solution)/shard_map/ppermute | solution.py:393
  169.4 2.4 %collective-permute-start.22 = (f32[2,128,256]{2,1,0:T(8,128)S(1)}, f32[2,128,256]{2,1,0:T(8,128)S(1)}, u32[]{:S(2)}, u32[]{:S(2)}) collective-permute-start(f32[2,128,256]{2,1,0:T(8,128)S(1)} %collective-permute-done.20.a0), channel_id=1, source_target_pairs={{0,1},{1,0},{2,3},{3,2},{4,5},{5,4},{6,7},{7,6},{8,9},{9,8},{10,11... | collective-permute-start | bytes 786440 | tf_op jit(solution)/shard_map/ppermute | solution.py:393
